TPU v7x, 32 devices: a whole 2x2x4 slice. The times are simulated.
32 devices in a mesh: grp: 2 (over y), row: 16 (over z, x, core), col: 1.
Axes of the slice: x: 2, y: 2, z: 4, core: 2. Of those that a mesh axis runs over, the one named last changes fastest.
Arguments:
- pair: bfloat16 [256, 128, 128], P(('grp', 'row'), 'col'), parts along dimension 0, may hold values from -6 to 6
- in_gain: float32 [2, 128], replicated, may hold values from 0.25 to 1.75
- in_shift: float32 [2, 128], replicated, may hold values from -3 to 3
- proj: bfloat16 [2, 128, 640], replicated, may hold values from -0.5 to 0.5
- out_gain: float32 [2, 128], replicated, may hold values from 0.25 to 1.75
- out_shift: float32 [2, 128], replicated, may hold values from -3 to 3
- out_weight: bfloat16 [2, 128, 128], replicated, may hold values from -0.5 to 0.5
Outputs:
- updated: bfloat16 [256, 128, 128], P(('grp', 'row'), 'col'), parts along dimension 0
There are 2 independent parts, one for each index of `grp`. A program takes and returns all parts, laid end to end along the dimension named above; an argument that names none is the same for every part. Nothing has to cross between parts.
All inputs are finite; a program needn't handle non-finite values.
Results may differ from a plain program's by a relative error of at most 0.013.
Values may be sent and summed in bfloat16 or wider, within the bound.
A program may use at most 64 MiB of HBM per device.

v0:
```python
import jax
import jax.numpy as jnp
from jax import lax
from jax.sharding import PartitionSpec as P


def layer_norm(values, scale_vec, offset, axis_pos):
    average = jnp.mean(values, axis=axis_pos, keepdims=True)
    centred = values - average
    variance = jnp.mean(centred * centred, axis=axis_pos, keepdims=True)
    return centred * lax.rsqrt(variance + 1e-05) * scale_vec + offset


def arrange_blocks(arrived, row_count, col_count):
    sources, local_chan, rows_here, cols_here = arrived.shape
    shaped = arrived.reshape(row_count, col_count, local_chan, rows_here, cols_here)
    shaped = shaped.transpose(2, 0, 3, 1, 4)
    return shaped.reshape(local_chan, row_count * rows_here, col_count * cols_here)


def body(pair, in_gain, in_shift, proj, out_gain, out_shift, out_weight):
    rows_here, cols_here, channels = pair.shape
    row_count = lax.axis_size("row")
    col_count = lax.axis_size("col")
    local_chan = channels // (row_count * col_count)
    current = pair
    for layer_index in range(2):
        normed = layer_norm(
            current.astype(jnp.float32), in_gain[layer_index], in_shift[layer_index], 2
        ).astype(jnp.bfloat16)
        weights = proj[layer_index]
        projected = jnp.einsum(
            "ijc,cd->dij", normed, weights[:, : 4 * channels], preferred_element_type=jnp.float32
        )
        left_edge = (
            jax.nn.sigmoid(projected[channels : 2 * channels]) * projected[:channels]
        ).astype(jnp.bfloat16)
        right_edge = (
            jax.nn.sigmoid(projected[3 * channels :]) * projected[2 * channels : 3 * channels]
        ).astype(jnp.bfloat16)
        out_gate = jax.nn.sigmoid(
            jnp.einsum(
                "ijc,cd->ijd",
                normed,
                weights[:, 4 * channels :],
                preferred_element_type=jnp.float32,
            )
        )
        left_arrived, right_arrived = (
            lax.all_to_all(
                left_edge[None], ("row", "col"), split_axis=1, concat_axis=0, tiled=True
            ),
            lax.all_to_all(
                right_edge[None], ("row", "col"), split_axis=1, concat_axis=0, tiled=True
            ),
        )
        left_full = arrange_blocks(left_arrived, row_count, col_count)
        right_full = arrange_blocks(right_arrived, row_count, col_count)
        if layer_index == 0:
            product = jnp.einsum(
                "cik,cjk->cij", left_full, right_full, preferred_element_type=jnp.float32
            )
        else:
            product = jnp.einsum(
                "cki,ckj->cij", left_full, right_full, preferred_element_type=jnp.float32
            )
        product = product.astype(jnp.bfloat16)
        outgoing = product.reshape(local_chan, row_count, rows_here, col_count, cols_here)
        outgoing = outgoing.transpose(1, 3, 0, 2, 4).reshape(
            row_count * col_count, local_chan, rows_here, cols_here
        )
        returned = lax.all_to_all(outgoing, ("row", "col"), split_axis=0, concat_axis=1, tiled=True)
        returned = returned.reshape(channels, rows_here, cols_here)
        product_norm = layer_norm(
            returned.astype(jnp.float32),
            out_gain[layer_index][:, None, None],
            out_shift[layer_index][:, None, None],
            0,
        ).astype(jnp.bfloat16)
        update = (
            jnp.einsum(
                "cij,cd->ijd",
                product_norm,
                out_weight[layer_index],
                preferred_element_type=jnp.float32,
            )
            * out_gate
        )
        current = (current.astype(jnp.float32) + update).astype(jnp.bfloat16)
    return current


def solution(mesh):
    placed = (P(("grp", "row"), "col", None), P(), P(), P(), P(), P(), P())
    return jax.shard_map(
        body, mesh=mesh, in_specs=placed, out_specs=P(("grp", "row"), "col", None), check_vma=False
    )
```

profile of v0, /device:TPU:0, one launch (start us, length us, event | category | flops | bytes accessed | tf_op | source)
XLA Modules:
  0.0 95.1 jit_solution(7251222842022501695)
XLA Ops:
  0.0 1.1 %copy.52 = bf16[8,128,128]{1,2,0:T(8,128)(2,1)S(1)} copy(bf16[8,128,128]{2,1,0:T(8,128)(2,1)} %param.7) | data formatting | bytes 524288 | tf_op args[0]
  1.3 1.0 %slice_bitcast_fusion = (bf16[128,640]{1,0:T(8,128)(2,1)S(1)}, bf16[128,640]{1,0:T(8,128)(2,1)S(1)}) fusion(bf16[2,128,640]{2,1,0:T(8,128)(2,1)} %param.10), kind=kLoop, calls=%fused_computation.87 | loop fusion | bytes 655360 | tf_op jit(solution)/shard_map/squeeze | solution.py:31
  2.3 0.8 slice_bitcast_fusion.10
  3.1 0.5 convolution_bitcast_fusion.1
  3.6 0.3 fusion.57
  3.9 0.9 copy.56
  4.8 7.4 %all-to-all-start.1 = ((bf16[1,128,8,128]{3,2,0,1:T(8,128)(2,1)}), bf16[1,128,8,128]{3,2,0,1:T(8,128)(2,1)S(1)}, u32[]{:S(2)}, u32[]{:S(2)}) async-start(bf16[1,128,8,128]{3,2,0,1:T(8,128)(2,1)} %copy.56), calls=%async_computation.1 | async-start | bytes 524288 | tf_op jit(solution)/shard_map/all_to_all | solution.py:53
  12.2 0.2 copy.54
  12.4 9.9 %all-to-all-done.1 = bf16[1,128,8,128]{3,2,0,1:T(8,128)(2,1)S(1)} async-done(((bf16[1,128,8,128]{3,2,0,1:T(8,128)(2,1)}), bf16[1,128,8,128]{3,2,0,1:T(8,128)(2,1)S(1)}, u32[]{:S(2)}, u32[]{:S(2)}) %all-to-all-start.1) | async-done | bytes 262176 | tf_op jit(solution)/shard_map/all_to_all | solution.py:53
  22.2 12.8 %all_to_all.24 = bf16[1,128,8,128]{3,2,0,1:T(8,128)(2,1)S(1)} all-to-all(bf16[1,128,8,128]{3,2,0,1:T(8,128)(2,1)S(1)} %copy.54), channel_id=1, replica_groups=mesh['grp'=2,'row'=16,'col'=1] {'row','col'}, dimensions={1} | all-to-all | bytes 524288 | tf_op jit(solution)/shard_map/all_to_all | solution.py:50
  35.0 0.3 fusion.11
  35.4 0.8 copy.110
  36.1 3.5 %all-to-all-start.2 = ((bf16[16,8,8,128]{3,2,1,0:T(8,128)(2,1)}), bf16[16,8,8,128]{3,2,1,0:T(8,128)(2,1)S(1)}, u32[]{:S(2)}, u32[]{:S(2)}) async-start(bf16[16,8,8,128]{3,2,1,0:T(8,128)(2,1)} %bitcast.86), calls=%async_computation.2 | async-start | bytes 524288 | tf_op jit(solution)/shard_map/all_to_all | solution.py:72
  39.9 0.4 fusion.5
  40.3 9.4 %all-to-all-done.2 = bf16[16,8,8,128]{3,2,1,0:T(8,128)(2,1)S(1)} async-done(((bf16[16,8,8,128]{3,2,1,0:T(8,128)(2,1)}), bf16[16,8,8,128]{3,2,1,0:T(8,128)(2,1)S(1)}, u32[]{:S(2)}, u32[]{:S(2)}) %all-to-all-start.2) | async-done | bytes 262176 | tf_op jit(solution)/shard_map/all_to_all | solution.py:72
  50.0 0.3 fusion.30
  50.3 0.3 fusion.67
  50.7 0.5 convolution_bitcast_fusion
  51.2 0.3 fusion.59
  51.5 0.9 copy.64
  52.4 3.5 %all-to-all-start.3 = ((bf16[1,128,8,128]{3,2,0,1:T(8,128)(2,1)}), bf16[1,128,8,128]{3,2,0,1:T(8,128)(2,1)S(1)}, u32[]{:S(2)}, u32[]{:S(2)}) async-start(bf16[1,128,8,128]{3,2,0,1:T(8,128)(2,1)} %copy.64), calls=%async_computation.3 | async-start | bytes 524288 | tf_op jit(solution)/shard_map/all_to_all | solution.py:50
  55.9 0.2 copy.66
  56.1 9.8 %all-to-all-done.3 = bf16[1,128,8,128]{3,2,0,1:T(8,128)(2,1)S(1)} async-done(((bf16[1,128,8,128]{3,2,0,1:T(8,128)(2,1)}), bf16[1,128,8,128]{3,2,0,1:T(8,128)(2,1)S(1)}, u32[]{:S(2)}, u32[]{:S(2)}) %all-to-all-start.3) | async-done | bytes 262176 | tf_op jit(solution)/shard_map/all_to_all | solution.py:50
  65.9 12.8 %all_to_all.25 = bf16[1,128,8,128]{3,2,0,1:T(8,128)(2,1)S(1)} all-to-all(bf16[1,128,8,128]{3,2,0,1:T(8,128)(2,1)S(1)} %copy.66), channel_id=1, replica_groups=mesh['grp'=2,'row'=16,'col'=1] {'row','col'}, dimensions={1} | all-to-all | bytes 524288 | tf_op jit(solution)/shard_map/all_to_all | solution.py:53
  78.8 0.3 fusion.12
  79.0 0.8 copy.109
  79.8 3.5 %all-to-all-start.5 = ((bf16[16,8,8,128]{3,2,1,0:T(8,128)(2,1)}), bf16[16,8,8,128]{3,2,1,0:T(8,128)(2,1)S(1)}, u32[]{:S(2)}, u32[]{:S(2)}) async-start(bf16[16,8,8,128]{3,2,1,0:T(8,128)(2,1)} %bitcast.85), calls=%async_computation.5 | async-start | bytes 524288 | tf_op jit(solution)/shard_map/all_to_all | solution.py:72
  83.5 0.4 fusion.2
  83.9 9.4 %all-to-all-done.5 = bf16[16,8,8,128]{3,2,1,0:T(8,128)(2,1)S(1)} async-done(((bf16[16,8,8,128]{3,2,1,0:T(8,128)(2,1)}), bf16[16,8,8,128]{3,2,1,0:T(8,128)(2,1)S(1)}, u32[]{:S(2)}, u32[]{:S(2)}) %all-to-all-start.5) | async-done | bytes 262176 | tf_op jit(solution)/shard_map/all_to_all | solution.py:72
  93.7 0.3 fusion.26
  94.0 0.3 fusion.10
  94.3 0.9 copy.74
  (26 shorter events, 1.2 us)
Async XLA Ops:
  3.9 35.7 %copy-start.1 = (f32[2,128]{1,0:T(2,128)S(1)}, f32[2,128]{1,0:T(2,128)}, u32[]{:S(2)}) copy-start(f32[2,128]{1,0:T(2,128)} %param.12) | copy-start | bytes 3076
  3.9 35.7 %copy-start.2 = (f32[2,128]{1,0:T(2,128)S(1)}, f32[2,128]{1,0:T(2,128)}, u32[]{:S(2)}) copy-start(f32[2,128]{1,0:T(2,128)} %param.11) | copy-start | bytes 3076
  4.8 17.4 %all-to-all-start.1 = ((bf16[1,128,8,128]{3,2,0,1:T(8,128)(2,1)}), bf16[1,128,8,128]{3,2,0,1:T(8,128)(2,1)S(1)}, u32[]{:S(2)}, u32[]{:S(2)}) async-start(bf16[1,128,8,128]{3,2,0,1:T(8,128)(2,1)} %copy.56), calls=%async_computation.1 | async-start | bytes 524288 | tf_op jit(solution)/shard_map/all_to_all | solution.py:53
  36.1 13.5 %all-to-all-start.2 = ((bf16[16,8,8,128]{3,2,1,0:T(8,128)(2,1)}), bf16[16,8,8,128]{3,2,1,0:T(8,128)(2,1)S(1)}, u32[]{:S(2)}, u32[]{:S(2)}) async-start(bf16[16,8,8,128]{3,2,1,0:T(8,128)(2,1)} %bitcast.86), calls=%async_computation.2 | async-start | bytes 524288 | tf_op jit(solution)/shard_map/all_to_all | solution.py:72
  39.7 10.6 %copy-start = (bf16[2,128,128]{2,1,0:T(8,128)(2,1)S(1)}, bf16[2,128,128]{2,1,0:T(8,128)(2,1)}, u32[]{:S(2)}) copy-start(bf16[2,128,128]{2,1,0:T(8,128)(2,1)} %param.13) | copy-start | bytes 196612
  52.4 13.5 %all-to-all-start.3 = ((bf16[1,128,8,128]{3,2,0,1:T(8,128)(2,1)}), bf16[1,128,8,128]{3,2,0,1:T(8,128)(2,1)S(1)}, u32[]{:S(2)}, u32[]{:S(2)}) async-start(bf16[1,128,8,128]{3,2,0,1:T(8,128)(2,1)} %copy.64), calls=%async_computation.3 | async-start | bytes 524288 | tf_op jit(solution)/shard_map/all_to_all | solution.py:50
  79.8 13.5 %all-to-all-start.5 = ((bf16[16,8,8,128]{3,2,1,0:T(8,128)(2,1)}), bf16[16,8,8,128]{3,2,1,0:T(8,128)(2,1)S(1)}, u32[]{:S(2)}, u32[]{:S(2)}) async-start(bf16[16,8,8,128]{3,2,1,0:T(8,128)(2,1)} %bitcast.85), calls=%async_computation.5 | async-start | bytes 524288 | tf_op jit(solution)/shard_map/all_to_all | solution.py:72
where the time goes:
time: 95.8 us; the launch traced here: 95.1 us
  waiting for transfers between devices  38.5 us (40%)
  blocking collectives  25.6 us (27%)
  starting transfers between devices  18 us (19%)
  local copies, waits for them, and re-layouts  7.81 us (8%)
  matrix products  3.01 us (3%)
  other arithmetic  2.04 us (2%)
    all_to_all x2, waiting for transfers between devices, body(): lax.all_to_all(outgoing, ('row', 'col'), split_axis=0, concat_axis=1, til...  18.8 us
    all_to_all x1, blocking collectives, body(): lax.all_to_all(right_edge[None], ('row', 'col'), split_axis=1, concat_axi...  12.8 us
    all_to_all x1, blocking collectives, body(): lax.all_to_all(left_edge[None], ('row', 'col'), split_axis=1, concat_axis...  12.8 us
    all_to_all x1, waiting for transfers between devices, body(): lax.all_to_all(right_edge[None], ('row', 'col'), split_axis=1, concat_axi...  9.85 us
    all_to_all x1, waiting for transfers between devices, body(): lax.all_to_all(left_edge[None], ('row', 'col'), split_axis=1, concat_axis...  9.81 us
    all_to_all x1, starting transfers between devices, body(): lax.all_to_all(right_edge[None], ('row', 'col'), split_axis=1, concat_axi...  7.36 us
    all_to_all x2, starting transfers between devices, body(): lax.all_to_all(outgoing, ('row', 'col'), split_axis=0, concat_axis=1, til...  7.07 us
    all_to_all x1, starting transfers between devices, body(): lax.all_to_all(left_edge[None], ('row', 'col'), split_axis=1, concat_axis...  3.53 us
  transfers between devices with their start and end apart: 4, of which 4 were waited for; matrix products, arithmetic and copies ran while one was open for 2% of the time, Pallas kernels for 0%

commit v1 on v0

--- a/solution.py
+++ b/solution.py
@@ -1,6 +1,10 @@
+import functools
+
 import jax
 import jax.numpy as jnp
 from jax import lax
+from jax.experimental import pallas as pl
+from jax.experimental.pallas import tpu as pltpu
 from jax.sharding import PartitionSpec as P
 
 
@@ -18,7 +22,7 @@
     return shaped.reshape(local_chan, row_count * rows_here, col_count * cols_here)
 
 
-def body(pair, in_gain, in_shift, proj, out_gain, out_shift, out_weight):
+def plain_body(pair, in_gain, in_shift, proj, out_gain, out_shift, out_weight):
     rows_here, cols_here, channels = pair.shape
     row_count = lax.axis_size("row")
     col_count = lax.axis_size("col")
@@ -90,6 +94,191 @@
     return current
 
 
+PARTS = 2
+TOKENS = 128
+CHANNELS = 128
+ROWS = 8
+
+
+def sigmoid(values):
+    return 0.5 * jnp.tanh(0.5 * values) + 0.5
+
+
+def kernel(
+    n, pair_ref, in_gain, in_shift, proj, out_gain, out_shift, out_weight, out_ref,
+    weights_t, normed, gate, current, edges, centred, send, recv, ret, got, send_sem, recv_sem,
+):
+    me = lax.axis_index("row")
+    part_chan = CHANNELS // PARTS
+    local = part_chan // n
+    cells = ROWS * TOKENS
+
+    def copy(layer, phase, part, source, target, offset):
+        dst = lax.rem(me + offset, n)
+        return pltpu.make_async_remote_copy(
+            src_ref=source.at[layer, part, dst],
+            dst_ref=target.at[layer, part, me],
+            send_sem=send_sem.at[layer, phase, part],
+            recv_sem=recv_sem.at[layer, phase, part],
+            device_id={"row": dst},
+            device_id_type=pl.DeviceIdType.MESH,
+        )
+
+    def start_all(layer, phase, part, source, target):
+        def step(offset, carry):
+            copy(layer, phase, part, source, target, offset).start()
+            return carry
+
+        lax.fori_loop(1, n, step, 0, unroll=True)
+        target[layer, part, me] = source[layer, part, me]
+
+    def wait_all(sems, layer, phase, part, buffer):
+        blocks = buffer.at[layer, part, pl.ds(0, n - 1)]
+        pltpu.make_async_copy(blocks, blocks, sems.at[layer, phase, part]).wait()
+
+    barrier = pltpu.get_barrier_semaphore()
+
+    def greet(offset, carry):
+        pl.semaphore_signal(
+            barrier, inc=1, device_id={"row": lax.rem(me + offset, n)},
+            device_id_type=pl.DeviceIdType.MESH,
+        )
+        return carry
+
+    lax.fori_loop(1, n, greet, 0)
+
+    for layer in range(2):
+        for block in range(4):
+            columns = proj[layer, :, block * CHANNELS : (block + 1) * CHANNELS]
+            turned = columns.astype(jnp.float32).T.astype(jnp.bfloat16)
+            for part in range(PARTS):
+                weights_t[layer, part, block * part_chan : (block + 1) * part_chan, :] = turned[
+                    part * part_chan : (part + 1) * part_chan
+                ]
+
+    for layer in range(2):
+        source = pair_ref if layer == 0 else current
+        for i in range(ROWS):
+            rows = source[i].astype(jnp.float32)
+            average = jnp.mean(rows, axis=-1, keepdims=True)
+            shifted = rows - average
+            variance = jnp.mean(shifted * shifted, axis=-1, keepdims=True)
+            normed[i] = (
+                shifted * lax.rsqrt(variance + 1e-05) * in_gain[layer][None] + in_shift[layer][None]
+            ).astype(jnp.bfloat16)
+        for part in range(PARTS):
+            for i in range(ROWS):
+                projected = lax.dot_general(
+                    weights_t[layer, part], normed[i], (((1,), (1,)), ((), ())),
+                    preferred_element_type=jnp.float32,
+                )
+                p1, p2, p3, p4 = (
+                    projected[b * part_chan : (b + 1) * part_chan] for b in range(4)
+                )
+                edges[part, pl.ds(i, part_chan, stride=2 * ROWS), :] = sigmoid(p2) * p1
+                edges[part, pl.ds(ROWS + i, part_chan, stride=2 * ROWS), :] = sigmoid(p4) * p3
+            send[layer, part] = (
+                edges[part].astype(jnp.bfloat16).reshape(n, local, 2 * ROWS, TOKENS)
+            )
+            if layer == 0 and part == 0:
+                pl.semaphore_wait(barrier, n - 1)
+            start_all(layer, 0, part, send, recv)
+        for i in range(ROWS):
+            gate[i] = sigmoid(
+                jnp.dot(
+                    normed[i], proj[layer, :, 4 * CHANNELS :], preferred_element_type=jnp.float32
+                )
+            )
+        for part in range(PARTS):
+            wait_all(recv_sem, layer, 0, part, recv)
+            for pair_at in range(local // 2):
+                products = []
+                for channel in (2 * pair_at, 2 * pair_at + 1):
+                    both = recv[layer, part, :, channel].astype(jnp.float32)
+                    left = both[:, :ROWS].reshape(TOKENS, TOKENS).astype(jnp.bfloat16)
+                    right = both[:, ROWS:].reshape(TOKENS, TOKENS).astype(jnp.bfloat16)
+                    dims = ((1,), (1,)) if layer == 0 else ((0,), (0,))
+                    product = lax.dot_general(
+                        left, right, (dims, ((), ())), preferred_element_type=jnp.float32
+                    )
+                    products.append(product.reshape(n, ROWS, TOKENS))
+                ret[layer, part, :, pair_at] = jnp.concatenate(products, axis=1).astype(
+                    jnp.bfloat16
+                )
+            start_all(layer, 1, part, ret, got)
+        total = jnp.zeros((ROWS, TOKENS), jnp.float32)
+        for part in range(PARTS):
+            wait_all(recv_sem, layer, 1, part, got)
+            values = got[layer, part].astype(jnp.float32).reshape(part_chan, ROWS, TOKENS)
+            first = part * part_chan * ROWS
+            centred[first : first + part_chan * ROWS] = values.reshape(part_chan * ROWS, TOKENS)
+            total += jnp.sum(values, axis=0)
+        average = total / CHANNELS
+        shifted = centred[...].reshape(CHANNELS, ROWS, TOKENS) - average[None]
+        variance = jnp.mean(shifted * shifted, axis=0)
+        scaled = shifted * lax.rsqrt(variance + 1e-05)[None]
+        centred[...] = scaled.reshape(CHANNELS * ROWS, TOKENS)
+        for i in range(ROWS):
+            turned = centred[pl.ds(i, CHANNELS, stride=ROWS), :].T
+            product_norm = (turned * out_gain[layer][None] + out_shift[layer][None]).astype(
+                jnp.bfloat16
+            )
+            update = (
+                jnp.dot(product_norm, out_weight[layer], preferred_element_type=jnp.float32)
+                * gate[i]
+            )
+            target = current if layer == 0 else out_ref
+            target[i] = (source[i].astype(jnp.float32) + update).astype(jnp.bfloat16)
+    for layer in range(2):
+        for part in range(PARTS):
+            wait_all(send_sem, layer, 0, part, send)
+            wait_all(send_sem, layer, 1, part, ret)
+
+
+def kernel_body(n, *arrays):
+    part_chan = CHANNELS // PARTS
+    local = part_chan // n
+    edge_blocks = (2, PARTS, n, local, 2 * ROWS, TOKENS)
+    product_blocks = (2, PARTS, n, local // 2, 2 * ROWS, TOKENS)
+    vmem = pl.BlockSpec(memory_space=pltpu.VMEM)
+    return pl.pallas_call(
+        functools.partial(kernel, n),
+        out_shape=jax.ShapeDtypeStruct((ROWS, TOKENS, CHANNELS), jnp.bfloat16),
+        in_specs=[vmem] * 7,
+        out_specs=vmem,
+        scratch_shapes=[
+            pltpu.VMEM((2, PARTS, 4 * part_chan, CHANNELS), jnp.bfloat16),
+            pltpu.VMEM((ROWS, TOKENS, CHANNELS), jnp.bfloat16),
+            pltpu.VMEM((ROWS, TOKENS, CHANNELS), jnp.float32),
+            pltpu.VMEM((ROWS, TOKENS, CHANNELS), jnp.bfloat16),
+            pltpu.VMEM((PARTS, part_chan * 2 * ROWS, TOKENS), jnp.float32),
+            pltpu.VMEM((CHANNELS * ROWS, TOKENS), jnp.float32),
+            pltpu.VMEM(edge_blocks, jnp.bfloat16),
+            pltpu.VMEM(edge_blocks, jnp.bfloat16),
+            pltpu.VMEM(product_blocks, jnp.bfloat16),
+            pltpu.VMEM(product_blocks, jnp.bfloat16),
+            pltpu.SemaphoreType.DMA((2, 2, PARTS)),
+            pltpu.SemaphoreType.DMA((2, 2, PARTS)),
+        ],
+        compiler_params=pltpu.CompilerParams(
+            collective_id=0, has_side_effects=True, vmem_limit_bytes=48 * 1024 * 1024
+        ),
+    )(*arrays)
+
+
+def body(pair, *params):
+    n = lax.axis_size("row")
+    fits = (
+        lax.axis_size("col") == 1
+        and pair.shape == (ROWS, TOKENS, CHANNELS)
+        and n * ROWS == TOKENS
+        and CHANNELS % (2 * n * PARTS) == 0
+    )
+    if fits:
+        return kernel_body(n, pair, *params)
+    return plain_body(pair, *params)
+
+
 def solution(mesh):
     placed = (P(("grp", "row"), "col", None), P(), P(), P(), P(), P(), P())
     return jax.shard_map(

time: 95.8 us -> 54 us (0.56)
  Pallas kernels: 0 us -> 47.5 us
  waiting for transfers between devices: 38.5 us -> 0 us
  blocking collectives: 25.6 us -> 0 us
  starting transfers between devices: 18 us -> 0 us
  matrix products: 3.01 us -> 0 us
  other arithmetic: 2.04 us -> 0 us
  local copies, waits for them, and re-layouts: 7.81 us -> 6.18 us
    pallas_call x0 -> x1, Pallas kernels: none -> 47.5 us  [kernel_body(): pl.pallas_call(functools.partial(kernel, n), out_shape=jax.ShapeDtypeStru...]
    all_to_all x4 -> x0, waiting for transfers between devices: 38.5 us -> none  [the longest x2 18.8 us: body(): lax.all_to_all(outgoing, ('row', 'col'), split_axis=0, concat_axis=1, til...]
    all_to_all x2 -> x0, blocking collectives: 25.6 us -> none  [the longest x1 12.8 us: body(): lax.all_to_all(right_edge[None], ('row', 'col'), split_axis=1, concat_axi...]
    all_to_all x4 -> x0, starting transfers between devices: 18 us -> none  [the longest x1 7.36 us: body(): lax.all_to_all(right_edge[None], ('row', 'col'), split_axis=1, concat_axi...]
    unnamed x7 -> x15, local copies, waits for them, and re-layouts: 1.14 us -> 6.18 us
    dot_general x8 -> x0, matrix products: 3.01 us -> none  [the longest x2 1.08 us: body(): jnp.einsum('ijc,cd->dij', normed, weights[:, :4 * channels], preferred_el...]
    broadcast_in_dim x4 -> x0, local copies, waits for them, and re-layouts: 2.14 us -> none  [the longest x2 1.07 us: body(): right_edge[None]]
    reshape x2 -> x0, local copies, waits for them, and re-layouts: 1.55 us -> none  [body(): product.reshape(local_chan, row_count, rows_here, col_count, cols_here)]
  transfers between devices with their start and end apart: 4 -> 0, of which waited for: 4 -> 0; matrix products, arithmetic and copies ran while one was open for 2% -> 0% of each run, Pallas kernels for 0% -> 0%
where the time goes in v1:
time: 54 us; the launch traced here: 53.7 us
  Pallas kernels  47.5 us (88%)
  local copies, waits for them, and re-layouts  6.18 us (11%)
    pallas_call x1, Pallas kernels, kernel_body(): pl.pallas_call(functools.partial(kernel, n), out_shape=jax.ShapeDtypeStru...  47.5 us
    unnamed x15, local copies, waits for them, and re-layouts  6.18 us

profile of v1, /device:TPU:0, one launch (start us, length us, event | category | flops | bytes accessed | tf_op | source)
XLA Modules:
  0.0 53.7 jit_solution(6830877503066254033)
XLA Ops:
  0.0 0.0 copy-start
  0.0 1.0 %copy-done = bf16[2,128,640]{2,1,0:T(8,128)(2,1)S(1)} copy-done((bf16[2,128,640]{2,1,0:T(8,128)(2,1)S(1)}, bf16[2,128,640]{2,1,0:T(8,128)(2,1)}, u32[]{:S(2)}) %copy-start) | copy-done | bytes 327704
  1.0 0.0 copy-start.1
  1.0 0.9 %copy-done.1 = bf16[8,128,128]{2,1,0:T(8,128)(2,1)S(1)} copy-done((bf16[8,128,128]{2,1,0:T(8,128)(2,1)S(1)}, bf16[8,128,128]{2,1,0:T(8,128)(2,1)}, u32[]{:S(2)}) %copy-start.1) | copy-done | bytes 262168
  1.9 0.0 copy-start.2
  1.9 0.8 %copy-done.2 = bf16[2,128,128]{2,1,0:T(8,128)(2,1)S(1)} copy-done((bf16[2,128,128]{2,1,0:T(8,128)(2,1)S(1)}, bf16[2,128,128]{2,1,0:T(8,128)(2,1)}, u32[]{:S(2)}) %copy-start.2) | copy-done | bytes 65560
  2.8 0.0 copy-start.3
  2.8 0.7 %copy-done.3 = f32[2,128]{1,0:T(2,128)S(1)} copy-done((f32[2,128]{1,0:T(2,128)S(1)}, f32[2,128]{1,0:T(2,128)}, u32[]{:S(2)}) %copy-start.3) | copy-done | bytes 1048
  3.4 0.0 copy-start.4
  3.4 0.7 %copy-done.4 = f32[2,128]{1,0:T(2,128)S(1)} copy-done((f32[2,128]{1,0:T(2,128)S(1)}, f32[2,128]{1,0:T(2,128)}, u32[]{:S(2)}) %copy-start.4) | copy-done | bytes 1048
  4.1 0.0 copy-start.5
  4.1 0.7 %copy-done.5 = f32[2,128]{1,0:T(2,128)S(1)} copy-done((f32[2,128]{1,0:T(2,128)S(1)}, f32[2,128]{1,0:T(2,128)}, u32[]{:S(2)}) %copy-start.5) | copy-done | bytes 1048
  4.8 0.0 copy-start.6
  4.8 0.7 %copy-done.6 = f32[2,128]{1,0:T(2,128)S(1)} copy-done((f32[2,128]{1,0:T(2,128)S(1)}, f32[2,128]{1,0:T(2,128)}, u32[]{:S(2)}) %copy-start.6) | copy-done | bytes 1048
  5.5 47.5 %shard_map.73 = bf16[8,128,128]{2,1,0:T(8,128)(2,1)S(1)} custom-call(bf16[8,128,128]{2,1,0:T(8,128)(2,1)S(1)} %copy-done.1, f32[2,128]{1,0:T(2,128)S(1)} %copy-done.3, f32[2,128]{1,0:T(2,128)S(1)} %copy-done.4, bf16[2,128,640]{2,1,0:T(8,128)(2,1)S(1)} %copy-done, f32[2,128]{1,0:T(2,128)S(1)} %copy-done.5, f32[2,128]{1,0:T(2,128)S(1)} %copy-done.6, ...), custom_call_target="tpu_custom_call" | custom-call | tf_op jit(solution)/shard_map/pallas_call | solution.py:244
  53.0 0.7 %copy.9 = bf16[8,128,128]{2,1,0:T(8,128)(2,1)} copy(bf16[8,128,128]{2,1,0:T(8,128)(2,1)S(1)} %shard_map.73) | data formatting | bytes 524288
Async XLA Ops:
  0.0 1.0 %copy-start = (bf16[2,128,640]{2,1,0:T(8,128)(2,1)S(1)}, bf16[2,128,640]{2,1,0:T(8,128)(2,1)}, u32[]{:S(2)}) copy-start(bf16[2,128,640]{2,1,0:T(8,128)(2,1)} %proj.1) | copy-start | bytes 983044
  1.0 0.9 %copy-start.1 = (bf16[8,128,128]{2,1,0:T(8,128)(2,1)S(1)}, bf16[8,128,128]{2,1,0:T(8,128)(2,1)}, u32[]{:S(2)}) copy-start(bf16[8,128,128]{2,1,0:T(8,128)(2,1)} %pair_ref.1) | copy-start | bytes 786436
  1.9 0.8 %copy-start.2 = (bf16[2,128,128]{2,1,0:T(8,128)(2,1)S(1)}, bf16[2,128,128]{2,1,0:T(8,128)(2,1)}, u32[]{:S(2)}) copy-start(bf16[2,128,128]{2,1,0:T(8,128)(2,1)} %out_weight.1) | copy-start | bytes 196612
  2.8 0.7 %copy-start.3 = (f32[2,128]{1,0:T(2,128)S(1)}, f32[2,128]{1,0:T(2,128)}, u32[]{:S(2)}) copy-start(f32[2,128]{1,0:T(2,128)} %in_gain.1) | copy-start | bytes 3076
  3.4 0.7 %copy-start.4 = (f32[2,128]{1,0:T(2,128)S(1)}, f32[2,128]{1,0:T(2,128)}, u32[]{:S(2)}) copy-start(f32[2,128]{1,0:T(2,128)} %in_shift.1) | copy-start | bytes 3076
  4.1 0.7 %copy-start.5 = (f32[2,128]{1,0:T(2,128)S(1)}, f32[2,128]{1,0:T(2,128)}, u32[]{:S(2)}) copy-start(f32[2,128]{1,0:T(2,128)} %out_gain.1) | copy-start | bytes 3076
  4.8 0.7 %copy-start.6 = (f32[2,128]{1,0:T(2,128)S(1)}, f32[2,128]{1,0:T(2,128)}, u32[]{:S(2)}) copy-start(f32[2,128]{1,0:T(2,128)} %out_shift.1) | copy-start | bytes 3076

commit v2 on v1

--- a/solution.py
+++ b/solution.py
@@ -94,7 +94,7 @@
     return current
 
 
-PARTS = 2
+PARTS = (1, 2)
 TOKENS = 128
 CHANNELS = 128
 ROWS = 8
@@ -104,37 +104,39 @@
     return 0.5 * jnp.tanh(0.5 * values) + 0.5
 
 
-def kernel(
-    n, pair_ref, in_gain, in_shift, proj, out_gain, out_shift, out_weight, out_ref,
-    weights_t, normed, gate, current, edges, centred, send, recv, ret, got, send_sem, recv_sem,
-):
+def kernel(n, *refs):
+    hbm, out_ref, vmem, rest = refs[:7], refs[7], refs[8:15], refs[15:]
+    pair_ref, in_gain, in_shift, proj, out_gain, out_shift, out_weight = vmem
+    load_sem, weights_t, normed, gate, current, edges, centred, send_sem, recv_sem = rest[:9]
+    buffers = rest[9:]
+    loads = [
+        pltpu.make_async_copy(hbm[at], vmem[at], load_sem.at[at]) for at in (0, 3, 1, 2, 4, 5, 6)
+    ]
+    for load in loads:
+        load.start()
     me = lax.axis_index("row")
-    part_chan = CHANNELS // PARTS
-    local = part_chan // n
-    cells = ROWS * TOKENS
-
-    def copy(layer, phase, part, source, target, offset):
-        dst = lax.rem(me + offset, n)
-        return pltpu.make_async_remote_copy(
-            src_ref=source.at[layer, part, dst],
-            dst_ref=target.at[layer, part, me],
-            send_sem=send_sem.at[layer, phase, part],
-            recv_sem=recv_sem.at[layer, phase, part],
-            device_id={"row": dst},
+    half = n // 2
+    side, place = me // half, lax.rem(me, half)
+
+    def start(source, target, sems, device):
+        pltpu.make_async_remote_copy(
+            src_ref=source,
+            dst_ref=target,
+            send_sem=send_sem.at[sems],
+            recv_sem=recv_sem.at[sems],
+            device_id={"row": device},
             device_id_type=pl.DeviceIdType.MESH,
-        )
-
-    def start_all(layer, phase, part, source, target):
-        def step(offset, carry):
-            copy(layer, phase, part, source, target, offset).start()
-            return carry
-
-        lax.fori_loop(1, n, step, 0, unroll=True)
-        target[layer, part, me] = source[layer, part, me]
-
-    def wait_all(sems, layer, phase, part, buffer):
-        blocks = buffer.at[layer, part, pl.ds(0, n - 1)]
-        pltpu.make_async_copy(blocks, blocks, sems.at[layer, phase, part]).wait()
+        ).start()
+
+    def start_half(source, target, sems, slot):
+        for offset in range(1, half):
+            other = lax.rem(place + offset, half)
+            start(source.at[other], target.at[slot], sems, side * half + other)
+        target[slot] = source[place]
+
+    def wait_all(sem, buffer, count):
+        blocks = buffer.at[pl.ds(0, count)]
+        pltpu.make_async_copy(blocks, blocks, sem).wait()
 
     barrier = pltpu.get_barrier_semaphore()
 
@@ -147,16 +149,23 @@
 
     lax.fori_loop(1, n, greet, 0)
 
+    loads[1].wait()
     for layer in range(2):
+        part_chan = CHANNELS // PARTS[layer]
         for block in range(4):
             columns = proj[layer, :, block * CHANNELS : (block + 1) * CHANNELS]
             turned = columns.astype(jnp.float32).T.astype(jnp.bfloat16)
-            for part in range(PARTS):
-                weights_t[layer, part, block * part_chan : (block + 1) * part_chan, :] = turned[
-                    part * part_chan : (part + 1) * part_chan
-                ]
-
+            for part in range(PARTS[layer]):
+                weights_t[
+                    layer, pl.ds((4 * part + block) * part_chan, part_chan), :
+                ] = turned[part * part_chan : (part + 1) * part_chan]
+    for load in (loads[0], loads[2], loads[3]):
+        load.wait()
     for layer in range(2):
+        parts = PARTS[layer]
+        part_chan = CHANNELS // parts
+        pairs = part_chan // half // 2
+        send, recv, ret, got = buffers[4 * layer : 4 * layer + 4]
         source = pair_ref if layer == 0 else current
         for i in range(ROWS):
             rows = source[i].astype(jnp.float32)
@@ -166,50 +175,78 @@
             normed[i] = (
                 shifted * lax.rsqrt(variance + 1e-05) * in_gain[layer][None] + in_shift[layer][None]
             ).astype(jnp.bfloat16)
-        for part in range(PARTS):
+        for part in range(parts):
             for i in range(ROWS):
                 projected = lax.dot_general(
-                    weights_t[layer, part], normed[i], (((1,), (1,)), ((), ())),
+                    weights_t[layer, pl.ds(4 * part * part_chan, 4 * part_chan), :],
+                    normed[i], (((1,), (1,)), ((), ())),
                     preferred_element_type=jnp.float32,
                 )
                 p1, p2, p3, p4 = (
                     projected[b * part_chan : (b + 1) * part_chan] for b in range(4)
                 )
-                edges[part, pl.ds(i, part_chan, stride=2 * ROWS), :] = sigmoid(p2) * p1
-                edges[part, pl.ds(ROWS + i, part_chan, stride=2 * ROWS), :] = sigmoid(p4) * p3
-            send[layer, part] = (
-                edges[part].astype(jnp.bfloat16).reshape(n, local, 2 * ROWS, TOKENS)
-            )
+                edges[0, pl.ds(i, part_chan, stride=ROWS), :] = sigmoid(p2) * p1
+                edges[1, pl.ds(i, part_chan, stride=ROWS), :] = sigmoid(p4) * p3
+            for edge in range(2):
+                send[part, :, edge] = (
+                    edges[edge, : part_chan * ROWS]
+                    .astype(jnp.bfloat16)
+                    .reshape(half, pairs, 2 * ROWS, TOKENS)
+                )
+            sems = (layer, 0, part)
             if layer == 0 and part == 0:
                 pl.semaphore_wait(barrier, n - 1)
-            start_all(layer, 0, part, send, recv)
+            if layer == 0:
+                for offset in range(half):
+                    other = lax.rem(place + offset, half)
+                    start(
+                        send.at[part, other, 1], recv.at[part, me, 1], sems,
+                        (1 - side) * half + other,
+                    )
+                start_half(send.at[part], recv.at[part], sems, me)
+            else:
+                start_half(send.at[part], recv.at[part], sems, place)
         for i in range(ROWS):
             gate[i] = sigmoid(
                 jnp.dot(
                     normed[i], proj[layer, :, 4 * CHANNELS :], preferred_element_type=jnp.float32
                 )
             )
-        for part in range(PARTS):
-            wait_all(recv_sem, layer, 0, part, recv)
-            for pair_at in range(local // 2):
+        for part in range(parts):
+            count = half // 2 + half - 1 if layer == 0 else half - 1
+            wait_all(recv_sem.at[layer, 0, part], recv.at[part], count)
+            own = pl.ds(side * half, half) if layer == 0 else slice(None)
+            for pair_at in range(pairs):
+                left = recv[part, own, 0, pair_at].astype(jnp.float32)
+                right = recv[part, :, 1, pair_at].astype(jnp.float32)
                 products = []
-                for channel in (2 * pair_at, 2 * pair_at + 1):
-                    both = recv[layer, part, :, channel].astype(jnp.float32)
-                    left = both[:, :ROWS].reshape(TOKENS, TOKENS).astype(jnp.bfloat16)
-                    right = both[:, ROWS:].reshape(TOKENS, TOKENS).astype(jnp.bfloat16)
-                    dims = ((1,), (1,)) if layer == 0 else ((0,), (0,))
+                for rows in (slice(0, ROWS), slice(ROWS, 2 * ROWS)):
                     product = lax.dot_general(
-                        left, right, (dims, ((), ())), preferred_element_type=jnp.float32
+                        left[:, rows].reshape(-1, TOKENS).astype(jnp.bfloat16),
+                        right[:, rows].reshape(-1, TOKENS).astype(jnp.bfloat16),
+                        (((1,), (1,)) if layer == 0 else ((0,), (0,)), ((), ())),
+                        preferred_element_type=jnp.float32,
                     )
-                    products.append(product.reshape(n, ROWS, TOKENS))
-                ret[layer, part, :, pair_at] = jnp.concatenate(products, axis=1).astype(
-                    jnp.bfloat16
-                )
-            start_all(layer, 1, part, ret, got)
+                    products.append(product.reshape(-1, ROWS, TOKENS))
+                ret[part, :, pair_at] = jnp.concatenate(products, axis=1).astype(jnp.bfloat16)
+            sems = (layer, 1, part)
+            if layer == 0:
+                start_half(ret.at[part], got.at[part], sems, place)
+            else:
+                for offset in range(1, n):
+                    other = lax.rem(me + offset, n)
+                    start(ret.at[part, other], got.at[part, me], sems, other)
+                got[part, me] = ret[part, me]
+        if layer == 0:
+            for load in loads[4:]:
+                load.wait()
         total = jnp.zeros((ROWS, TOKENS), jnp.float32)
-        for part in range(PARTS):
-            wait_all(recv_sem, layer, 1, part, got)
-            values = got[layer, part].astype(jnp.float32).reshape(part_chan, ROWS, TOKENS)
+        for part in range(parts):
+            wait_all(recv_sem.at[layer, 1, part], got.at[part], (half if layer == 0 else n) - 1)
+            values = got[part].astype(jnp.float32)
+            if layer == 1:
+                values = values[:half] + values[half:]
+            values = values.reshape(part_chan, ROWS, TOKENS)
             first = part * part_chan * ROWS
             centred[first : first + part_chan * ROWS] = values.reshape(part_chan * ROWS, TOKENS)
             total += jnp.sum(values, axis=0)
@@ -230,39 +267,44 @@
             target = current if layer == 0 else out_ref
             target[i] = (source[i].astype(jnp.float32) + update).astype(jnp.bfloat16)
     for layer in range(2):
-        for part in range(PARTS):
-            wait_all(send_sem, layer, 0, part, send)
-            wait_all(send_sem, layer, 1, part, ret)
+        send, recv, ret, got = buffers[4 * layer : 4 * layer + 4]
+        for part in range(PARTS[layer]):
+            count = half // 2 + half - 1 if layer == 0 else half - 1
+            wait_all(send_sem.at[layer, 0, part], recv.at[part], count)
+            wait_all(send_sem.at[layer, 1, part], got.at[part], (half if layer == 0 else n) - 1)
 
 
 def kernel_body(n, *arrays):
-    part_chan = CHANNELS // PARTS
-    local = part_chan // n
-    edge_blocks = (2, PARTS, n, local, 2 * ROWS, TOKENS)
-    product_blocks = (2, PARTS, n, local // 2, 2 * ROWS, TOKENS)
-    vmem = pl.BlockSpec(memory_space=pltpu.VMEM)
+    half = n // 2
+    blocks = []
+    for layer in range(2):
+        parts = PARTS[layer]
+        tiles = (CHANNELS // parts // half // 2, 2 * ROWS, TOKENS)
+        blocks += [
+            (parts, half, 2) + tiles,
+            (parts, n if layer == 0 else half, 2) + tiles,
+            (parts, half if layer == 0 else n) + tiles,
+            (parts, half if layer == 0 else n) + tiles,
+        ]
     return pl.pallas_call(
         functools.partial(kernel, n),
         out_shape=jax.ShapeDtypeStruct((ROWS, TOKENS, CHANNELS), jnp.bfloat16),
-        in_specs=[vmem] * 7,
-        out_specs=vmem,
-        scratch_shapes=[
-            pltpu.VMEM((2, PARTS, 4 * part_chan, CHANNELS), jnp.bfloat16),
+        in_specs=[pl.BlockSpec(memory_space=pltpu.HBM)] * 7,
+        out_specs=pl.BlockSpec(memory_space=pltpu.VMEM),
+        scratch_shapes=[pltpu.VMEM(array.shape, array.dtype) for array in arrays]
+        + [
+            pltpu.SemaphoreType.DMA((7,)),
+            pltpu.VMEM((2, 4 * CHANNELS, CHANNELS), jnp.bfloat16),
             pltpu.VMEM((ROWS, TOKENS, CHANNELS), jnp.bfloat16),
             pltpu.VMEM((ROWS, TOKENS, CHANNELS), jnp.float32),
             pltpu.VMEM((ROWS, TOKENS, CHANNELS), jnp.bfloat16),
-            pltpu.VMEM((PARTS, part_chan * 2 * ROWS, TOKENS), jnp.float32),
+            pltpu.VMEM((2, CHANNELS * ROWS, TOKENS), jnp.float32),
             pltpu.VMEM((CHANNELS * ROWS, TOKENS), jnp.float32),
-            pltpu.VMEM(edge_blocks, jnp.bfloat16),
-            pltpu.VMEM(edge_blocks, jnp.bfloat16),
-            pltpu.VMEM(product_blocks, jnp.bfloat16),
-            pltpu.VMEM(product_blocks, jnp.bfloat16),
-            pltpu.SemaphoreType.DMA((2, 2, PARTS)),
-            pltpu.SemaphoreType.DMA((2, 2, PARTS)),
-        ],
-        compiler_params=pltpu.CompilerParams(
-            collective_id=0, has_side_effects=True, vmem_limit_bytes=48 * 1024 * 1024
-        ),
+            pltpu.SemaphoreType.DMA((2, 2, max(PARTS))),
+            pltpu.SemaphoreType.DMA((2, 2, max(PARTS))),
+        ]
+        + [pltpu.VMEM(block, jnp.bfloat16) for block in blocks],
+        compiler_params=pltpu.CompilerParams(collective_id=0, has_side_effects=True),
     )(*arrays)
 
 
@@ -272,7 +314,8 @@
         lax.axis_size("col") == 1
         and pair.shape == (ROWS, TOKENS, CHANNELS)
         and n * ROWS == TOKENS
-        and CHANNELS % (2 * n * PARTS) == 0
+        and n % 4 == 0
+        and all(CHANNELS % (n * parts) == 0 for parts in PARTS)
     )
     if fits:
         return kernel_body(n, pair, *params)

time: 54 us -> 46.3 us (0.86)
  local copies, waits for them, and re-layouts: 6.18 us -> 1.67 us
  Pallas kernels: 47.5 us -> 44.5 us
    unnamed x15 -> x1, local copies, waits for them, and re-layouts: 6.18 us -> 1.67 us
    pallas_call x1, Pallas kernels: 47.5 us -> 44.5 us  [kernel_body(): pl.pallas_call(functools.partial(kernel, n), out_shape=jax.ShapeDtypeStru...]
where the time goes in v2:
time: 46.3 us; the launch traced here: 46.2 us
  Pallas kernels  44.5 us (96%)
  local copies, waits for them, and re-layouts  1.67 us (4%)
    pallas_call x1, Pallas kernels, kernel_body(): pl.pallas_call(functools.partial(kernel, n), out_shape=jax.ShapeDtypeStru...  44.5 us
    unnamed x1, local copies, waits for them, and re-layouts  1.67 us

profile of v2, /device:TPU:0, one launch (start us, length us, event | category | flops | bytes accessed | tf_op | source)
XLA Modules:
  0.0 46.2 jit_solution(6028314487481410291)
XLA Ops:
  0.0 44.5 %shard_map.73 = bf16[8,128,128]{2,1,0:T(8,128)(2,1)} custom-call(bf16[8,128,128]{2,1,0:T(8,128)(2,1)} %refs_0_.1, f32[2,128]{1,0:T(2,128)} %refs_1_.1, f32[2,128]{1,0:T(2,128)} %refs_2_.1, bf16[2,128,640]{2,1,0:T(8,128)(2,1)} %refs_3_.1, f32[2,128]{1,0:T(2,128)} %refs_4_.1, f32[2,128]{1,0:T(2,128)} %refs_5_.1, bf16[2,128,128]{2,1,0:T(8,128)(2,1)} %refs_6_.1), custom_call_target="tpu_custom_call" | custom-call | tf_op jit(solution)/shard_map/pallas_call | solution.py:289
  44.5 1.7 %copy.9 = bf16[8,128,128]{2,1,0:T(8,128)(2,1)} copy(bf16[8,128,128]{2,1,0:T(8,128)(2,1)} %shard_map.73) | data formatting | bytes 524288

commit v3 on v2

--- a/solution.py
+++ b/solution.py
@@ -94,7 +94,7 @@
     return current
 
 
-PARTS = (1, 2)
+PARTS = ((("half", 96), ("half", 32)), (("half", 64), ("all", 64)))
 TOKENS = 128
 CHANNELS = 128
 ROWS = 8
@@ -108,12 +108,10 @@
     hbm, out_ref, vmem, rest = refs[:7], refs[7], refs[8:15], refs[15:]
     pair_ref, in_gain, in_shift, proj, out_gain, out_shift, out_weight = vmem
     load_sem, weights_t, normed, gate, current, edges, centred, send_sem, recv_sem = rest[:9]
-    buffers = rest[9:]
-    loads = [
-        pltpu.make_async_copy(hbm[at], vmem[at], load_sem.at[at]) for at in (0, 3, 1, 2, 4, 5, 6)
-    ]
-    for load in loads:
-        load.start()
+    buffers, at = [], 9
+    for layer in range(2):
+        buffers.append([rest[at + 4 * part : at + 4 * part + 4] for part in range(len(PARTS[layer]))])
+        at += 4 * len(PARTS[layer])
     me = lax.axis_index("row")
     half = n // 2
     side, place = me // half, lax.rem(me, half)
@@ -128,6 +126,12 @@
             device_id_type=pl.DeviceIdType.MESH,
         ).start()
 
+    def start_group(source, target, sems):
+        for offset in range(1, n):
+            other = lax.rem(me + offset, n)
+            start(source.at[other], target.at[me], sems, other)
+        target[me] = source[me]
+
     def start_half(source, target, sems, slot):
         for offset in range(1, half):
             other = lax.rem(place + offset, half)
@@ -138,6 +142,24 @@
         blocks = buffer.at[pl.ds(0, count)]
         pltpu.make_async_copy(blocks, blocks, sem).wait()
 
+    def arriving(layer, kind):
+        if kind == "all":
+            return n - 1, n - 1
+        return (half // 2 + half - 1, half - 1) if layer == 0 else (half - 1, n - 1)
+
+    def start_edges(layer, part):
+        send, recv, _, _ = buffers[layer][part]
+        sems = (layer, 0, part)
+        if PARTS[layer][part][0] == "all":
+            start_group(send, recv, sems)
+        elif layer == 0:
+            for offset in range(half):
+                other = lax.rem(place + offset, half)
+                start(send.at[other, 1], recv.at[me, 1], sems, (1 - side) * half + other)
+            start_half(send, recv, sems, me)
+        else:
+            start_half(send, recv, sems, place)
+
     barrier = pltpu.get_barrier_semaphore()
 
     def greet(offset, carry):
@@ -148,24 +170,27 @@
         return carry
 
     lax.fori_loop(1, n, greet, 0)
+    loads = [
+        pltpu.make_async_copy(hbm[at], vmem[at], load_sem.at[at]) for at in (0, 3, 1, 2, 4, 5, 6)
+    ]
+    for load in loads:
+        load.start()
 
     loads[1].wait()
     for layer in range(2):
-        part_chan = CHANNELS // PARTS[layer]
         for block in range(4):
             columns = proj[layer, :, block * CHANNELS : (block + 1) * CHANNELS]
             turned = columns.astype(jnp.float32).T.astype(jnp.bfloat16)
-            for part in range(PARTS[layer]):
-                weights_t[
-                    layer, pl.ds((4 * part + block) * part_chan, part_chan), :
-                ] = turned[part * part_chan : (part + 1) * part_chan]
+            first = 0
+            for _, count in PARTS[layer]:
+                weights_t[layer, pl.ds(4 * first + block * count, count), :] = turned[
+                    first : first + count
+                ]
+                first += count
     for load in (loads[0], loads[2], loads[3]):
         load.wait()
     for layer in range(2):
         parts = PARTS[layer]
-        part_chan = CHANNELS // parts
-        pairs = part_chan // half // 2
-        send, recv, ret, got = buffers[4 * layer : 4 * layer + 4]
         source = pair_ref if layer == 0 else current
         for i in range(ROWS):
             rows = source[i].astype(jnp.float32)
@@ -175,50 +200,44 @@
             normed[i] = (
                 shifted * lax.rsqrt(variance + 1e-05) * in_gain[layer][None] + in_shift[layer][None]
             ).astype(jnp.bfloat16)
-        for part in range(parts):
+        first = 0
+        for part, (kind, count) in enumerate(parts):
+            send, recv, ret, got = buffers[layer][part]
             for i in range(ROWS):
                 projected = lax.dot_general(
-                    weights_t[layer, pl.ds(4 * part * part_chan, 4 * part_chan), :],
+                    weights_t[layer, pl.ds(4 * first, 4 * count), :],
                     normed[i], (((1,), (1,)), ((), ())),
                     preferred_element_type=jnp.float32,
                 )
-                p1, p2, p3, p4 = (
-                    projected[b * part_chan : (b + 1) * part_chan] for b in range(4)
+                p1, p2, p3, p4 = (projected[b * count : (b + 1) * count] for b in range(4))
+                edges[0, pl.ds(i, count, stride=ROWS), :] = sigmoid(p2) * p1
+                edges[1, pl.ds(i, count, stride=ROWS), :] = sigmoid(p4) * p3
+            for edge in range(2):
+                send[:, edge] = (
+                    edges[edge, : count * ROWS]
+                    .astype(jnp.bfloat16)
+                    .reshape(send.shape[0], send.shape[2], 2 * ROWS, TOKENS)
                 )
-                edges[0, pl.ds(i, part_chan, stride=ROWS), :] = sigmoid(p2) * p1
-                edges[1, pl.ds(i, part_chan, stride=ROWS), :] = sigmoid(p4) * p3
-            for edge in range(2):
-                send[part, :, edge] = (
-                    edges[edge, : part_chan * ROWS]
-                    .astype(jnp.bfloat16)
-                    .reshape(half, pairs, 2 * ROWS, TOKENS)
-                )
-            sems = (layer, 0, part)
-            if layer == 0 and part == 0:
-                pl.semaphore_wait(barrier, n - 1)
-            if layer == 0:
-                for offset in range(half):
-                    other = lax.rem(place + offset, half)
-                    start(
-                        send.at[part, other, 1], recv.at[part, me, 1], sems,
-                        (1 - side) * half + other,
-                    )
-                start_half(send.at[part], recv.at[part], sems, me)
-            else:
-                start_half(send.at[part], recv.at[part], sems, place)
+            if layer == 1:
+                start_edges(layer, part)
+            first += count
         for i in range(ROWS):
             gate[i] = sigmoid(
                 jnp.dot(
                     normed[i], proj[layer, :, 4 * CHANNELS :], preferred_element_type=jnp.float32
                 )
             )
-        for part in range(parts):
-            count = half // 2 + half - 1 if layer == 0 else half - 1
-            wait_all(recv_sem.at[layer, 0, part], recv.at[part], count)
-            own = pl.ds(side * half, half) if layer == 0 else slice(None)
-            for pair_at in range(pairs):
-                left = recv[part, own, 0, pair_at].astype(jnp.float32)
-                right = recv[part, :, 1, pair_at].astype(jnp.float32)
+        if layer == 0:
+            pl.semaphore_wait(barrier, n - 1)
+            for part in range(len(parts)):
+                start_edges(layer, part)
+        for part, (kind, count) in enumerate(parts):
+            send, recv, ret, got = buffers[layer][part]
+            wait_all(recv_sem.at[layer, 0, part], recv, arriving(layer, kind)[0])
+            own = pl.ds(side * half, half) if (layer, kind) == (0, "half") else slice(None)
+            for pair_at in range(send.shape[2]):
+                left = recv[own, 0, pair_at].astype(jnp.float32)
+                right = recv[:, 1, pair_at].astype(jnp.float32)
                 products = []
                 for rows in (slice(0, ROWS), slice(ROWS, 2 * ROWS)):
                     product = lax.dot_general(
@@ -228,28 +247,26 @@
                         preferred_element_type=jnp.float32,
                     )
                     products.append(product.reshape(-1, ROWS, TOKENS))
-                ret[part, :, pair_at] = jnp.concatenate(products, axis=1).astype(jnp.bfloat16)
-            sems = (layer, 1, part)
-            if layer == 0:
-                start_half(ret.at[part], got.at[part], sems, place)
+                ret[:, pair_at] = jnp.concatenate(products, axis=1).astype(jnp.bfloat16)
+            if (layer, kind) == (0, "half"):
+                start_half(ret, got, (layer, 1, part), place)
             else:
-                for offset in range(1, n):
-                    other = lax.rem(me + offset, n)
-                    start(ret.at[part, other], got.at[part, me], sems, other)
-                got[part, me] = ret[part, me]
+                start_group(ret, got, (layer, 1, part))
         if layer == 0:
             for load in loads[4:]:
                 load.wait()
         total = jnp.zeros((ROWS, TOKENS), jnp.float32)
-        for part in range(parts):
-            wait_all(recv_sem.at[layer, 1, part], got.at[part], (half if layer == 0 else n) - 1)
-            values = got[part].astype(jnp.float32)
-            if layer == 1:
+        first = 0
+        for part, (kind, count) in enumerate(parts):
+            got = buffers[layer][part][3]
+            wait_all(recv_sem.at[layer, 1, part], got, arriving(layer, kind)[1])
+            values = got[...].astype(jnp.float32)
+            if (layer, kind) == (1, "half"):
                 values = values[:half] + values[half:]
-            values = values.reshape(part_chan, ROWS, TOKENS)
-            first = part * part_chan * ROWS
-            centred[first : first + part_chan * ROWS] = values.reshape(part_chan * ROWS, TOKENS)
-            total += jnp.sum(values, axis=0)
+            values = values.reshape(count * ROWS, TOKENS)
+            centred[first * ROWS : (first + count) * ROWS] = values
+            total += jnp.sum(values.reshape(count, ROWS, TOKENS), axis=0)
+            first += count
         average = total / CHANNELS
         shifted = centred[...].reshape(CHANNELS, ROWS, TOKENS) - average[None]
         variance = jnp.mean(shifted * shifted, axis=0)
@@ -267,25 +284,22 @@
             target = current if layer == 0 else out_ref
             target[i] = (source[i].astype(jnp.float32) + update).astype(jnp.bfloat16)
     for layer in range(2):
-        send, recv, ret, got = buffers[4 * layer : 4 * layer + 4]
-        for part in range(PARTS[layer]):
-            count = half // 2 + half - 1 if layer == 0 else half - 1
-            wait_all(send_sem.at[layer, 0, part], recv.at[part], count)
-            wait_all(send_sem.at[layer, 1, part], got.at[part], (half if layer == 0 else n) - 1)
+        for part, (kind, _) in enumerate(PARTS[layer]):
+            send, recv, ret, got = buffers[layer][part]
+            wait_all(send_sem.at[layer, 0, part], recv, arriving(layer, kind)[0])
+            wait_all(send_sem.at[layer, 1, part], got, arriving(layer, kind)[1])
 
 
 def kernel_body(n, *arrays):
     half = n // 2
     blocks = []
     for layer in range(2):
-        parts = PARTS[layer]
-        tiles = (CHANNELS // parts // half // 2, 2 * ROWS, TOKENS)
-        blocks += [
-            (parts, half, 2) + tiles,
-            (parts, n if layer == 0 else half, 2) + tiles,
-            (parts, half if layer == 0 else n) + tiles,
-            (parts, half if layer == 0 else n) + tiles,
-        ]
+        for kind, count in PARTS[layer]:
+            owners = half if kind == "half" else n
+            sources = half if (layer, kind) == (1, "half") else n
+            rows = half if (layer, kind) == (0, "half") else n
+            tiles = (count // owners // 2, 2 * ROWS, TOKENS)
+            blocks += [(owners, 2) + tiles, (sources, 2) + tiles, (rows,) + tiles, (rows,) + tiles]
     return pl.pallas_call(
         functools.partial(kernel, n),
         out_shape=jax.ShapeDtypeStruct((ROWS, TOKENS, CHANNELS), jnp.bfloat16),
@@ -300,8 +314,8 @@
             pltpu.VMEM((ROWS, TOKENS, CHANNELS), jnp.bfloat16),
             pltpu.VMEM((2, CHANNELS * ROWS, TOKENS), jnp.float32),
             pltpu.VMEM((CHANNELS * ROWS, TOKENS), jnp.float32),
-            pltpu.SemaphoreType.DMA((2, 2, max(PARTS))),
-            pltpu.SemaphoreType.DMA((2, 2, max(PARTS))),
+            pltpu.SemaphoreType.DMA((2, 2, max(len(parts) for parts in PARTS))),
+            pltpu.SemaphoreType.DMA((2, 2, max(len(parts) for parts in PARTS))),
         ]
         + [pltpu.VMEM(block, jnp.bfloat16) for block in blocks],
         compiler_params=pltpu.CompilerParams(collective_id=0, has_side_effects=True),
@@ -315,7 +329,11 @@
         and pair.shape == (ROWS, TOKENS, CHANNELS)
         and n * ROWS == TOKENS
         and n % 4 == 0
-        and all(CHANNELS % (n * parts) == 0 for parts in PARTS)
+        and all(
+            count % (2 * (n if kind == "all" else n // 2)) == 0
+            for parts in PARTS
+            for kind, count in parts
+        )
     )
     if fits:
         return kernel_body(n, pair, *params)

time: 46.3 us -> 42.9 us (0.927)
  Pallas kernels: 44.5 us -> 41.1 us
    pallas_call x1, Pallas kernels: 44.5 us -> 41.1 us  [kernel_body(): pl.pallas_call(functools.partial(kernel, n), out_shape=jax.ShapeDtypeStru...]
where the time goes in v3:
time: 42.9 us; the launch traced here: 42.7 us
  Pallas kernels  41.1 us (96%)
  local copies, waits for them, and re-layouts  1.67 us (4%)
    pallas_call x1, Pallas kernels, kernel_body(): pl.pallas_call(functools.partial(kernel, n), out_shape=jax.ShapeDtypeStru...  41.1 us
    unnamed x1, local copies, waits for them, and re-layouts  1.67 us

profile of v3, /device:TPU:0, one launch (start us, length us, event | category | flops | bytes accessed | tf_op | source)
XLA Modules:
  0.0 42.7 jit_solution(14331370891607157768)
XLA Ops:
  0.0 41.1 %shard_map.73 = bf16[8,128,128]{2,1,0:T(8,128)(2,1)} custom-call(bf16[8,128,128]{2,1,0:T(8,128)(2,1)} %refs_0_.1, f32[2,128]{1,0:T(2,128)} %refs_1_.1, f32[2,128]{1,0:T(2,128)} %refs_2_.1, bf16[2,128,640]{2,1,0:T(8,128)(2,1)} %refs_3_.1, f32[2,128]{1,0:T(2,128)} %refs_4_.1, f32[2,128]{1,0:T(2,128)} %refs_5_.1, bf16[2,128,128]{2,1,0:T(8,128)(2,1)} %refs_6_.1), custom_call_target="tpu_custom_call" | custom-call | tf_op jit(solution)/shard_map/pallas_call | solution.py:303
  41.1 1.7 %copy.9 = bf16[8,128,128]{2,1,0:T(8,128)(2,1)} copy(bf16[8,128,128]{2,1,0:T(8,128)(2,1)} %shard_map.73) | data formatting | bytes 524288

commit v4 on v3

--- a/solution.py
+++ b/solution.py
@@ -154,7 +154,7 @@
             start_group(send, recv, sems)
         elif layer == 0:
             for offset in range(half):
-                other = lax.rem(place + offset, half)
+                other = lax.rem(place + offset + 2, half)
                 start(send.at[other, 1], recv.at[me, 1], sems, (1 - side) * half + other)
             start_half(send, recv, sems, me)
         else:
@@ -169,7 +169,7 @@
         )
         return carry
 
-    lax.fori_loop(1, n, greet, 0)
+    lax.fori_loop(1, n, greet, 0, unroll=True)
     loads = [
         pltpu.make_async_copy(hbm[at], vmem[at], load_sem.at[at]) for at in (0, 3, 1, 2, 4, 5, 6)
     ]

time: 42.9 us -> 42.7 us (level)
  no operation moved by 1% of the time
where the time goes in v4:
time: 42.7 us; the launch traced here: 42.5 us
  Pallas kernels  40.8 us (96%)
  local copies, waits for them, and re-layouts  1.67 us (4%)
    pallas_call x1, Pallas kernels, kernel_body(): pl.pallas_call(functools.partial(kernel, n), out_shape=jax.ShapeDtypeStru...  40.8 us
    unnamed x1, local copies, waits for them, and re-layouts  1.67 us

profile of v4, /device:TPU:0, one launch (start us, length us, event | category | flops | bytes accessed | tf_op | source)
XLA Modules:
  0.0 42.5 jit_solution(17933056860510712334)
XLA Ops:
  0.0 40.8 %shard_map.73 = bf16[8,128,128]{2,1,0:T(8,128)(2,1)} custom-call(bf16[8,128,128]{2,1,0:T(8,128)(2,1)} %refs_0_.1, f32[2,128]{1,0:T(2,128)} %refs_1_.1, f32[2,128]{1,0:T(2,128)} %refs_2_.1, bf16[2,128,640]{2,1,0:T(8,128)(2,1)} %refs_3_.1, f32[2,128]{1,0:T(2,128)} %refs_4_.1, f32[2,128]{1,0:T(2,128)} %refs_5_.1, bf16[2,128,128]{2,1,0:T(8,128)(2,1)} %refs_6_.1), custom_call_target="tpu_custom_call" | custom-call | tf_op jit(solution)/shard_map/pallas_call | solution.py:303
  40.8 1.7 %copy.9 = bf16[8,128,128]{2,1,0:T(8,128)(2,1)} copy(bf16[8,128,128]{2,1,0:T(8,128)(2,1)} %shard_map.73) | data formatting | bytes 524288

commit v5 on v4

--- a/solution.py
+++ b/solution.py
@@ -133,7 +133,7 @@
         target[me] = source[me]
 
     def start_half(source, target, sems, slot):
-        for offset in range(1, half):
+        for offset in (2, 3, 4, 5, 6, 7, 1):
             other = lax.rem(place + offset, half)
             start(source.at[other], target.at[slot], sems, side * half + other)
         target[slot] = source[place]

time: 42.7 us -> 42.6 us (level)
  no operation moved by 1% of the time
where the time goes in v5:
time: 42.6 us; the launch traced here: 42.5 us
  Pallas kernels  40.8 us (96%)
  local copies, waits for them, and re-layouts  1.67 us (4%)
    pallas_call x1, Pallas kernels, kernel_body(): pl.pallas_call(functools.partial(kernel, n), out_shape=jax.ShapeDtypeStru...  40.8 us
    unnamed x1, local copies, waits for them, and re-layouts  1.67 us

profile of v5, /device:TPU:0, one launch (start us, length us, event | category | flops | bytes accessed | tf_op | source)
XLA Modules:
  0.0 42.5 jit_solution(12890112401479561640)
XLA Ops:
  0.0 40.8 %shard_map.73 = bf16[8,128,128]{2,1,0:T(8,128)(2,1)} custom-call(bf16[8,128,128]{2,1,0:T(8,128)(2,1)} %refs_0_.1, f32[2,128]{1,0:T(2,128)} %refs_1_.1, f32[2,128]{1,0:T(2,128)} %refs_2_.1, bf16[2,128,640]{2,1,0:T(8,128)(2,1)} %refs_3_.1, f32[2,128]{1,0:T(2,128)} %refs_4_.1, f32[2,128]{1,0:T(2,128)} %refs_5_.1, bf16[2,128,128]{2,1,0:T(8,128)(2,1)} %refs_6_.1), custom_call_target="tpu_custom_call" | custom-call | tf_op jit(solution)/shard_map/pallas_call | solution.py:303
  40.8 1.7 %copy.9 = bf16[8,128,128]{2,1,0:T(8,128)(2,1)} copy(bf16[8,128,128]{2,1,0:T(8,128)(2,1)} %shard_map.73) | data formatting | bytes 524288
